TPU v7x, 512 devices: a whole 4x4x16 slice. The times are simulated.
512 devices in a mesh: row: 32 (over y, x, core), col: 16 (over z).
Axes of the slice: x: 4, y: 4, z: 16, core: 2. Of those that a mesh axis runs over, the one named last changes fastest.
Arguments:
- matrix: float32 [12288, 12288], P('row', 'col'), may hold values from -10 to 10, as said below
- panel: float32 [12288, 64], P('row'), may hold values from -1.12763724 to 1.12763724
Outputs:
- updated: float32 [12288, 12288], P('row', 'col')
- band_block: float32 [64, 64], replicated
Inputs may be any that keep to these rules, and one draw needn't show every extreme that they name: matrix is exactly symmetric.
All inputs are finite; a program needn't handle non-finite values.
Results may differ from a plain program's by a relative error of at most 0.0002.
Values sent between devices are 32-bit elements; how exact they have to be, the bound alone decides.
A program may use at most 64 MiB of HBM per device.

v0:
```python
import jax
import jax.numpy as jnp
from jax import lax
from jax.sharding import PartitionSpec as P

precise = lax.Precision.HIGHEST


def partner_2(block, axis, stride):
    count = lax.axis_size(axis)
    route = []
    for low in range(count):
        high = low | 1 << stride
        if high != low and high < count:
            route += [(low, high), (high, low)]
    return lax.ppermute(block, axis, route)


def from_root(value, axis, source):
    kept = jnp.where(lax.axis_index(axis) == source, value, 0).astype(value.dtype)
    return lax.psum(kept, axis)


def upper_cholesky(gram_block):
    order_now = gram_block.shape[0]
    positions = jnp.arange(order_now)

    def one_column(column_index, lower_part):
        gram_column = lax.dynamic_slice_in_dim(gram_block, column_index, 1, 1)[:, 0]
        lower_row = lax.dynamic_slice_in_dim(lower_part, column_index, 1, 0)[0]
        earlier = jnp.where(positions < column_index, lower_row, 0.0)
        reduced = gram_column - jnp.dot(lower_part, earlier, precision=precise)
        pivot_value = jnp.sum(jnp.where(positions == column_index, reduced, 0.0))
        diagonal_value = jnp.sqrt(pivot_value)
        new_column = jnp.where(positions > column_index, reduced / diagonal_value, 0.0) + jnp.where(
            positions == column_index, diagonal_value, 0.0
        )
        return jnp.where(positions[None, :] == column_index, new_column[:, None], lower_part)

    lower_part = lax.fori_loop(
        0, order_now, one_column, jnp.zeros((order_now, order_now), jnp.float32)
    )
    return lower_part.T


def upper_inverse(upper_block):
    order_now = upper_block.shape[0]
    positions = jnp.arange(order_now)

    def one_row(step_count, inverse_part):
        row_at = order_now - 1 - step_count
        upper_row = lax.dynamic_slice_in_dim(upper_block, row_at, 1, 0)[0]
        diagonal_value = jnp.sum(jnp.where(positions == row_at, upper_row, 0.0))
        beyond = jnp.where(positions > row_at, upper_row, 0.0)
        unit_row = jnp.where(positions == row_at, 1.0, 0.0)
        new_row = (unit_row - jnp.dot(beyond, inverse_part, precision=precise)) / diagonal_value
        return jnp.where(positions[:, None] == row_at, new_row[None, :], inverse_part)

    return lax.fori_loop(0, order_now, one_row, jnp.zeros((order_now, order_now), jnp.float32))


def small_factor(block_in):
    order_now = block_in.shape[0]
    positions = jnp.arange(order_now)

    def one_pivot(pivot_index, state_pair):
        working, lower_whole = state_pair
        pivot_column = lax.dynamic_slice_in_dim(working, pivot_index, 1, 1)[:, 0]
        pivot_row = lax.dynamic_slice_in_dim(working, pivot_index, 1, 0)[0]
        pivot_value = jnp.sum(jnp.where(positions == pivot_index, pivot_column, 0.0))
        multipliers = jnp.where(positions > pivot_index, pivot_column / pivot_value, 0.0)
        lower_whole = lower_whole + multipliers[:, None] * (
            positions[None, :] == pivot_index
        ).astype(jnp.float32)
        working = working - multipliers[:, None] * pivot_row[None, :]
        return (working, lower_whole)

    working, lower_whole = lax.fori_loop(
        0, order_now, one_pivot, (block_in, jnp.eye(order_now, dtype=jnp.float32))
    )
    return (lower_whole, jnp.triu(working))


def body(matrix, panel):
    local_rows, local_columns = matrix.shape
    panel_width = panel.shape[1]
    row_index = lax.axis_index("row")
    current_column_index = lax.axis_index("col")
    local_inner = jnp.dot(panel.T, panel, precision=precise)
    head_rows = panel[:panel_width]
    band_factor = -upper_cholesky(local_inner)
    levels = lax.axis_size("row").bit_length() - 1
    for bit_level in range(levels):
        partner = partner_2(band_factor, "row", bit_level)
        keeps_first = row_index >> bit_level & 1 == 0
        earlier_one = jnp.where(keeps_first, band_factor, partner)
        later_one = jnp.where(keeps_first, partner, band_factor)
        paired = jnp.dot(earlier_one.T, earlier_one, precision=precise) + jnp.dot(
            later_one.T, later_one, precision=precise
        )
        band_factor = -upper_cholesky(paired)
    head_rows = from_root(head_rows, "row", 0)
    factor_inverse = upper_inverse(band_factor)
    orthogonal_rows = jnp.dot(panel, factor_inverse, precision=precise)
    orthogonal_head = jnp.dot(head_rows, factor_inverse, precision=precise)
    identity = jnp.eye(panel_width, dtype=jnp.float32)
    lower_whole, upper_whole = small_factor(orthogonal_head - identity)
    global_rows = row_index * local_rows + jnp.arange(local_rows)
    unit_rows = (global_rows[:, None] == jnp.arange(panel_width)[None, :]).astype(jnp.float32)
    reflect_rows = jnp.dot(
        orthogonal_rows - unit_rows, upper_inverse(upper_whole), precision=precise
    )
    triangle = -jnp.dot(upper_whole, upper_inverse(lower_whole.T), precision=precise)
    gathered_reflect = lax.all_gather(reflect_rows, "row", axis=0, tiled=True)
    reflect_columns = lax.dynamic_slice_in_dim(
        gathered_reflect, current_column_index * local_columns, local_columns, 0
    )
    partial_product = lax.dot_general(
        matrix, reflect_rows, (((0,), (0,)), ((), ())), precision=precise
    )
    product = lax.psum(partial_product, "row")
    applied_cols = jnp.dot(product, triangle, precision=precise)
    inner_part = jnp.dot(reflect_columns.T, applied_cols, precision=precise)
    inner_total = lax.psum(inner_part, "col")
    coupling = jnp.dot(triangle.T, inner_total, precision=precise)
    corrected_cols = applied_cols - 0.5 * jnp.dot(reflect_columns, coupling, precision=precise)
    gathered_corrected = lax.all_gather(corrected_cols, "col", axis=0, tiled=True)
    corrected_rows = lax.dynamic_slice_in_dim(
        gathered_corrected, row_index * local_rows, local_rows, 0
    )
    left_factor = jnp.concatenate([reflect_rows, corrected_rows], 1)
    right_factor = jnp.concatenate([corrected_cols, reflect_columns], 1)
    updated = matrix - lax.dot_general(
        left_factor, right_factor, (((1,), (1,)), ((), ())), precision=precise
    )
    return (updated, band_factor)


def solution(mesh):
    return jax.shard_map(
        body,
        mesh=mesh,
        in_specs=(P("row", "col"), P("row", None)),
        out_specs=(P("row", "col"), P()),
        check_vma=False,
    )
```

profile of v0, /device:TPU:14, one launch (start us, length us, event | category | flops | bytes accessed | tf_op | source)
XLA Modules:
  0.0 1399.8 jit_solution(851780001571916975)
XLA Ops:
  7.2 1.2 fusion.154
  8.5 101.3 %while.159 = (s32[]{:T(128)}, f32[64,64]{1,0:T(8,128)S(1)}, f32[64,64]{0,1:T(8,128)S(1)}, s32[]{:T(128)}, s32[]{:T(128)}) while((s32[]{:T(128)}, f32[64,64]{1,0:T(8,128)S(1)}, f32[64,64]{0,1:T(8,128)S(1)}, s32[]{:T(128)}, s32[]{:T(128)}) %tuple.367), condition=%wide.region_2.3_spmd.clone.clone, body=%wide.region_0.2_spmd.clone.clone.sunk | while | flops 62274 | bytes 102632 | solution.py:40
  109.8 1.9 collective-permute-start
  111.9 1.1 collective-permute-done
  113.4 101.3 %while.160 = (s32[]{:T(128)}, f32[64,64]{1,0:T(8,128)S(1)}, f32[64,64]{0,1:T(8,128)S(1)}, s32[]{:T(128)}, s32[]{:T(128)}) while((s32[]{:T(128)}, f32[64,64]{1,0:T(8,128)S(1)}, f32[64,64]{0,1:T(8,128)S(1)}, s32[]{:T(128)}, s32[]{:T(128)}) %tuple.370), condition=%wide.region_5.6_spmd.clone.clone, body=%wide.region_3.5_spmd.clone.clone.sunk | while | flops 62274 | bytes 102632 | solution.py:40
  214.7 2.7 collective-permute-start.1
  217.5 3.0 collective-permute-done.1
  220.9 101.3 %while.161 = (s32[]{:T(128)}, f32[64,64]{1,0:T(8,128)S(1)}, f32[64,64]{0,1:T(8,128)S(1)}, s32[]{:T(128)}, s32[]{:T(128)}) while((s32[]{:T(128)}, f32[64,64]{1,0:T(8,128)S(1)}, f32[64,64]{0,1:T(8,128)S(1)}, s32[]{:T(128)}, s32[]{:T(128)}) %tuple.373), condition=%wide.region_8.9_spmd.clone.clone, body=%wide.region_6.8_spmd.clone.clone.sunk | while | flops 62274 | bytes 102632 | solution.py:40
  322.3 3.3 collective-permute-start.2
  325.6 4.0 collective-permute-done.2
  330.1 101.3 %while.162 = (s32[]{:T(128)}, f32[64,64]{1,0:T(8,128)S(1)}, f32[64,64]{0,1:T(8,128)S(1)}, s32[]{:T(128)}, s32[]{:T(128)}) while((s32[]{:T(128)}, f32[64,64]{1,0:T(8,128)S(1)}, f32[64,64]{0,1:T(8,128)S(1)}, s32[]{:T(128)}, s32[]{:T(128)}) %tuple.376), condition=%wide.region_11.12_spmd.clone.clone, body=%wide.region_9.11_spmd.clone.clone.sunk | while | flops 62274 | bytes 102632 | solution.py:40
  431.4 4.1 collective-permute-start.3
  435.5 1.8 collective-permute-done.3
  437.9 101.3 %while.163 = (s32[]{:T(128)}, f32[64,64]{1,0:T(8,128)S(1)}, f32[64,64]{0,1:T(8,128)S(1)}, s32[]{:T(128)}, s32[]{:T(128)}) while((s32[]{:T(128)}, f32[64,64]{1,0:T(8,128)S(1)}, f32[64,64]{0,1:T(8,128)S(1)}, s32[]{:T(128)}, s32[]{:T(128)}) %tuple.379), condition=%wide.region_14.15_spmd.clone.clone, body=%wide.region_12.14_spmd.clone.clone.sunk | while | flops 62274 | bytes 102632 | solution.py:40
  539.2 4.0 collective-permute-start.4
  543.3 102.9 %psum.21 = f32[64,64]{1,0:T(8,128)S(1)} all-reduce(f32[64,64]{1,0:T(8,128)S(1)} %broadcast_select_fusion.12), channel_id=1, replica_groups=mesh['row'=32,'col'=16] {'row'}, use_global_device_ids=true, to_apply=%region_21.22 | all-reduce | flops 4096 | bytes 32768 | tf_op jit(solution)/shard_map/psum | solution.py:21
  646.6 102.2 %while.164 = (s32[]{:T(128)}, f32[64,64]{1,0:T(8,128)S(1)}, f32[64,64]{0,1:T(8,128)S(1)}, s32[]{:T(128)}, s32[]{:T(128)}) while((s32[]{:T(128)}, f32[64,64]{1,0:T(8,128)S(1)}, f32[64,64]{0,1:T(8,128)S(1)}, s32[]{:T(128)}, s32[]{:T(128)}) %tuple.382), condition=%wide.region_17.18_spmd.clone.clone, body=%wide.region_15.17_spmd.clone.clone.sunk | while | flops 62274 | bytes 102632 | solution.py:40
  749.0 95.1 %while.165 = (s32[]{:T(128)}, f32[64,64]{1,0:T(8,128)S(1)}, f32[64,64]{1,0:T(8,128)S(1)}, s32[]{:T(128)}, s32[]{:T(128)}, /*index=5*/s32[]{:T(128)}, s32[]{:T(128)}) while((s32[]{:T(128)}, f32[64,64]{1,0:T(8,128)S(1)}, f32[64,64]{1,0:T(8,128)S(1)}, s32[]{:T(128)}, s32[]{:T(128)}, /*index=5*/s32[]{:T(128)}, ...), condition=%wide.region_20.21_spmd.clone.clone, body=%wide.region_18.20_spmd.clone.clone.sunk | while | flops 62086 | bytes 69153 | solution.py:59
  844.3 100.7 %while.158 = (s32[]{:T(128)}, f32[64,64]{0,1:T(8,128)S(1)}, f32[64,64]{0,1:T(8,128)S(1)}, s32[]{:T(128)}) while((s32[]{:T(128)}, f32[64,64]{0,1:T(8,128)S(1)}, f32[64,64]{0,1:T(8,128)S(1)}, s32[]{:T(128)}) %tuple.388), condition=%wide.region_24.25_spmd.clone.clone, body=%wide.region_22.24_spmd.clone.clone.sunk | while | flops 16897 | bytes 69965 | solution.py:78
  945.1 95.1 %while.166 = (s32[]{:T(128)}, f32[64,64]{1,0:T(8,128)S(1)}, f32[64,64]{1,0:T(8,128)S(1)}, s32[]{:T(128)}, s32[]{:T(128)}, /*index=5*/s32[]{:T(128)}, s32[]{:T(128)}) while((s32[]{:T(128)}, f32[64,64]{1,0:T(8,128)S(1)}, f32[64,64]{1,0:T(8,128)S(1)}, s32[]{:T(128)}, s32[]{:T(128)}, /*index=5*/s32[]{:T(128)}, ...), condition=%wide.region_27.28_spmd.clone.clone, body=%wide.region_25.27_spmd.clone.clone.sunk | while | flops 62086 | bytes 69153 | solution.py:59
  1040.8 1.5 convolution_bitcast_fusion.9
  1043.2 103.2 %while.167 = (s32[]{:T(128)}, f32[64,64]{1,0:T(8,128)S(1)}, f32[64,64]{1,0:T(8,128)S(1)}, s32[]{:T(128)}, s32[]{:T(128)}, /*index=5*/s32[]{:T(128)}, s32[]{:T(128)}) while((s32[]{:T(128)}, f32[64,64]{1,0:T(8,128)S(1)}, f32[64,64]{1,0:T(8,128)S(1)}, s32[]{:T(128)}, s32[]{:T(128)}, /*index=5*/s32[]{:T(128)}, ...), condition=%wide.region_31.32_spmd.clone.clone, body=%wide.region_29.31_spmd.clone.clone.sunk | while | flops 62086 | bytes 69153 | solution.py:59
  1116.4 0.8 fusion.236
  1146.5 45.9 %all-reduce.2.cloned.1.call-done = f32[768,64]{0,1:T(8,128)} async-done(((f32[768,64]{0,1:T(8,128)}), f32[768,64]{0,1:T(8,128)}) %all-reduce.2.cloned.1.call-update) | async-done | bytes 196624 | tf_op jit(solution)/shard_map/psum | solution.py:121
  1192.4 1.3 fusion.156
  1193.7 62.0 %all-gather.3.cloned.1.call-done = f32[12288,64]{0,1:T(8,128)} async-done(((f32[384,64]{0,1:T(8,128)}), f32[12288,64]{0,1:T(8,128)}) %all-gather.3.cloned.1.call-update) | async-done | bytes 3145744 | tf_op jit(solution)/shard_map/all_gather | solution.py:114
  1255.6 0.9 constant_dynamic-slice_fusion.8
  1256.9 56.9 %psum.23 = f32[64,64]{1,0:T(8,128)S(1)} all-reduce(f32[64,64]{1,0:T(8,128)S(1)} %fusion.157), channel_id=1, replica_groups=mesh['row'=32,'col'=16] {'col'}, use_global_device_ids=true, to_apply=%region_32.33 | all-reduce | flops 4096 | bytes 32768 | tf_op jit(solution)/shard_map/psum | solution.py:124
  1314.0 1.0 fusion.118
  1315.1 74.2 %all-gather.5.cloned.1.call-done = f32[12288,64]{0,1:T(8,128)} async-done(((f32[768,64]{0,1:T(8,128)}), f32[12288,64]{0,1:T(8,128)}) %all-gather.5.cloned.1.call-update) | async-done | bytes 3145744 | tf_op jit(solution)/shard_map/all_gather | solution.py:127
  1389.3 0.9 constant_dynamic-slice_fusion.7
  1390.2 3.1 convolution_subtract_fusion
  (3072 shorter events, 729.9 us)
Async XLA Ops:
  7.2 104.6 %slice-start = ((f32[384,64]{0,1:T(8,128)}), f32[64,64]{0,1:T(8,128)S(1)}, s32[]{:S(2)}) async-start(f32[384,64]{0,1:T(8,128)} %param.23), calls=%async_computation.3 | async-start | bytes 65536 | tf_op jit(solution)/shard_map/slice | solution.py:90
  7.2 1185.2 %all-reduce.2.cloned.1.call-start = ((), (), s32[]{:S(2)}) async-start(), calls=%async_computation | async-start | bytes 393216 | tf_op jit(solution)/shard_map/psum | solution.py:121
  109.8 3.1 collective-permute-start
  214.7 5.8 collective-permute-start.1
  322.3 7.3 collective-permute-start.2
  431.4 6.0 collective-permute-start.3
  539.2 107.0 %collective-permute-start.4 = (f32[64,64]{0,1:T(8,128)S(1)}, f32[64,64]{0,1:T(8,128)S(1)}, u32[]{:S(2)}, u32[]{:S(2)}) collective-permute-start(f32[64,64]{0,1:T(8,128)S(1)} %negate_bitcast_fusion.1), channel_id=1, source_target_pairs={{0,256},{256,0},{16,272},{272,16},{32,288},{288,32},{48,304},{304,... | collective-permute-start | bytes 49160 | tf_op jit(solution)/shard_map/ppermute | solution.py:16
  748.9 291.3 %copy-start.3 = (f32[384,64]{0,1:T(8,128)S(1)}, f32[384,64]{0,1:T(8,128)}, u32[]{:S(2)}) copy-start(f32[384,64]{0,1:T(8,128)} %param.23) | copy-start | bytes 294916
  749.0 291.9 %copy-start = (f32[384,768]{1,0:T(8,128)S(1)}, f32[384,768]{1,0:T(8,128)}, u32[]{:S(2)}) copy-start(f32[384,768]{1,0:T(8,128)} %param.22) | copy-start | bytes 3538948
  844.1 196.8 %copy-start.4 = (f32[64,64]{1,0:T(8,128)}, f32[64,64]{1,0:T(8,128)S(1)}, u32[]{:S(2)}) copy-start(f32[64,64]{1,0:T(8,128)S(1)} %get-tuple-element.1720) | copy-start | bytes 49156
  1040.8 1.6 copy-start.1
  1042.4 213.3 %all-gather.3.cloned.1.call-start = ((), (), s32[]{:S(2)}) async-start(), calls=%async_computation.1 | async-start | bytes 3244032 | tf_op jit(solution)/shard_map/all_gather | solution.py:114
  1043.1 346.2 %all-gather.5.cloned.1.call-start = ((), (), s32[]{:S(2)}) async-start(), calls=%async_computation.2 | async-start | bytes 3342336 | tf_op jit(solution)/shard_map/all_gather | solution.py:127
  1146.5 243.7 %copy-start.2 = (f32[384,64]{0,1:T(8,128)S(1)}, f32[384,64]{0,1:T(8,128)}, u32[]{:S(2)}) copy-start(f32[384,64]{0,1:T(8,128)} %copy-done.1) | copy-start | bytes 294916
Sparse Core Ops, SparseCore 0:
  1042.5 149.8 all-reduce.1
  1196.1 59.4 all-gather.2
  1315.2 74.0 all-gather.4
where the time goes:
time: 1410 us; the launch traced here: 1400 us
  matrix products  464 us (33%)
  loops' own time  277 us (20%)
  other arithmetic  262 us (19%)
  waiting for transfers between devices  193 us (14%)
  blocking collectives  160 us (11%)
  starting transfers between devices  16.2 us (1%)
  between operations  14.2 us (1%)
    dot_general x384, matrix products, one_column(): reduced = gram_column - jnp.dot(lower_part, earlier, precision=precise)  299 us
    another operation x6, loops' own time, upper_cholesky(): lax.fori_loop(0, order_now, one_column, jnp.zeros((order_now, order_now),...  274 us
    dot_general x192, matrix products, one_row(): jnp.dot(beyond, inverse_part, precision=precise)  154 us
    reduce_sum x192, other arithmetic, one_row(): diagonal_value = jnp.sum(jnp.where(positions == row_at, upper_row, 0.0))  123 us
    psum x1, blocking collectives, from_root(): return lax.psum(kept, axis)  103 us
    all_gather x1, waiting for transfers between devices, body(): lax.all_gather(corrected_cols, 'col', axis=0, tiled=True)  74.2 us
    all_gather x1, waiting for transfers between devices, body(): gathered_reflect = lax.all_gather(reflect_rows, 'row', axis=0, tiled=True)  62 us
    psum x1, blocking collectives, body(): inner_total = lax.psum(inner_part, 'col')  56.9 us
  transfers between devices with their start and end apart: 8, of which 7 were waited for; matrix products, arithmetic and copies ran while one was open for 7% of the time, Pallas kernels for 0%

commit v1 on v0

--- a/solution.py
+++ b/solution.py
@@ -1,9 +1,27 @@
+import functools
 import jax
 import jax.numpy as jnp
 from jax import lax
 from jax.sharding import PartitionSpec as P
+from jax.lax import axis_size, ppermute
 
 precise = lax.Precision.HIGHEST
+
+
+def obtain_files(x_part, link_axis):
+    n_chips = axis_size(link_axis)
+
+    def track_trails(r2, even):
+        if even >= n_chips:
+            return r2
+        return track_trails(
+            r2 + ppermute(r2, link_axis, [(w, w ^ even) for w in range(n_chips)]), 2 * even
+        )
+
+    return track_trails(x_part, 1)
+
+
+fill_threads_in = functools.partial(obtain_files, link_axis="col")
 
 
 def partner_2(block, axis, stride):
@@ -121,7 +139,7 @@
     product = lax.psum(partial_product, "row")
     applied_cols = jnp.dot(product, triangle, precision=precise)
     inner_part = jnp.dot(reflect_columns.T, applied_cols, precision=precise)
-    inner_total = lax.psum(inner_part, "col")
+    inner_total = fill_threads_in(inner_part)
     coupling = jnp.dot(triangle.T, inner_total, precision=precise)
     corrected_cols = applied_cols - 0.5 * jnp.dot(reflect_columns, coupling, precision=precise)
     gathered_corrected = lax.all_gather(corrected_cols, "col", axis=0, tiled=True)

time: 1410 us -> 1380 us (0.979)
  blocking collectives: 160 us -> 103 us
  starting transfers between devices: 16.2 us -> 45.8 us
  waiting for transfers between devices: 193 us -> 209 us
    psum x1 -> x0, blocking collectives: 56.9 us -> none  [body(): inner_total = lax.psum(inner_part, 'col')]
    ppermute x0 -> x4, starting transfers between devices: none -> 29.6 us  [track_trails(): ppermute(r2, link_axis, [(w, w ^ even) for w in range(n_chips)])]
  transfers between devices with their start and end apart: 8 -> 12, of which waited for: 7 -> 11; matrix products, arithmetic and copies ran while one was open for 7% -> 7% of each run, Pallas kernels for 0% -> 0%
where the time goes in v1:
time: 1380 us
  matrix products  458 us (33%)
  loops' own time  272 us (20%)
  other arithmetic  261 us (19%)
  waiting for transfers between devices  209 us (15%)
  blocking collectives  103 us (7%)
  starting transfers between devices  45.8 us (3%)
  between operations  14.3 us (1%)
  local copies, waits for them, and re-layouts  13.9 us (1%)
    dot_general x384, matrix products, one_column(): reduced = gram_column - jnp.dot(lower_part, earlier, precision=precise)  297 us
    another operation x6, loops' own time, upper_cholesky(): lax.fori_loop(0, order_now, one_column, jnp.zeros((order_now, order_now),...  269 us
    dot_general x192, matrix products, one_row(): jnp.dot(beyond, inverse_part, precision=precise)  150 us
    reduce_sum x192, other arithmetic, one_row(): diagonal_value = jnp.sum(jnp.where(positions == row_at, upper_row, 0.0))  122 us
    psum x1, blocking collectives, from_root(): return lax.psum(kept, axis)  103 us
    all_gather x1, waiting for transfers between devices, body(): lax.all_gather(corrected_cols, 'col', axis=0, tiled=True)  77.7 us
    all_gather x1, waiting for transfers between devices, body(): gathered_reflect = lax.all_gather(reflect_rows, 'row', axis=0, tiled=True)  62 us
    psum x1, waiting for transfers between devices, body(): product = lax.psum(partial_product, 'row')  50.3 us
  transfers between devices with their start and end apart: 12, of which 11 were waited for; matrix products, arithmetic and copies ran while one was open for 7% of the time, Pallas kernels for 0%

profile of v1, /device:TPU:14, one launch (start us, length us, event | category | flops | bytes accessed | tf_op | source)
XLA Modules:
  0.0 1377.6 jit_solution(17804076295393093456)
XLA Ops:
  8.5 101.3 %while.159 = (s32[]{:T(128)}, f32[64,64]{1,0:T(8,128)S(1)}, f32[64,64]{0,1:T(8,128)S(1)}, s32[]{:T(128)}, s32[]{:T(128)}) while((s32[]{:T(128)}, f32[64,64]{1,0:T(8,128)S(1)}, f32[64,64]{0,1:T(8,128)S(1)}, s32[]{:T(128)}, s32[]{:T(128)}) %tuple.367), condition=%wide.region_2.3_spmd.clone.clone, body=%wide.region_0.2_spmd.clone.clone.sunk | while | flops 62274 | bytes 102632 | solution.py:58
  109.8 1.9 collective-permute-start
  113.4 101.3 %while.160 = (s32[]{:T(128)}, f32[64,64]{1,0:T(8,128)S(1)}, f32[64,64]{0,1:T(8,128)S(1)}, s32[]{:T(128)}, s32[]{:T(128)}) while((s32[]{:T(128)}, f32[64,64]{1,0:T(8,128)S(1)}, f32[64,64]{0,1:T(8,128)S(1)}, s32[]{:T(128)}, s32[]{:T(128)}) %tuple.370), condition=%wide.region_5.6_spmd.clone.clone, body=%wide.region_3.5_spmd.clone.clone.sunk | while | flops 62274 | bytes 102632 | solution.py:58
  214.7 2.7 collective-permute-start.1
  217.5 3.0 collective-permute-done.1
  220.9 101.3 %while.161 = (s32[]{:T(128)}, f32[64,64]{1,0:T(8,128)S(1)}, f32[64,64]{0,1:T(8,128)S(1)}, s32[]{:T(128)}, s32[]{:T(128)}) while((s32[]{:T(128)}, f32[64,64]{1,0:T(8,128)S(1)}, f32[64,64]{0,1:T(8,128)S(1)}, s32[]{:T(128)}, s32[]{:T(128)}) %tuple.373), condition=%wide.region_8.9_spmd.clone.clone, body=%wide.region_6.8_spmd.clone.clone.sunk | while | flops 62274 | bytes 102632 | solution.py:58
  322.3 3.3 collective-permute-start.2
  325.6 4.0 collective-permute-done.2
  330.1 101.3 %while.162 = (s32[]{:T(128)}, f32[64,64]{1,0:T(8,128)S(1)}, f32[64,64]{0,1:T(8,128)S(1)}, s32[]{:T(128)}, s32[]{:T(128)}) while((s32[]{:T(128)}, f32[64,64]{1,0:T(8,128)S(1)}, f32[64,64]{0,1:T(8,128)S(1)}, s32[]{:T(128)}, s32[]{:T(128)}) %tuple.376), condition=%wide.region_11.12_spmd.clone.clone, body=%wide.region_9.11_spmd.clone.clone.sunk | while | flops 62274 | bytes 102632 | solution.py:58
  431.4 4.1 collective-permute-start.3
  435.5 1.8 collective-permute-done.3
  437.9 101.3 %while.163 = (s32[]{:T(128)}, f32[64,64]{1,0:T(8,128)S(1)}, f32[64,64]{0,1:T(8,128)S(1)}, s32[]{:T(128)}, s32[]{:T(128)}) while((s32[]{:T(128)}, f32[64,64]{1,0:T(8,128)S(1)}, f32[64,64]{0,1:T(8,128)S(1)}, s32[]{:T(128)}, s32[]{:T(128)}) %tuple.379), condition=%wide.region_14.15_spmd.clone.clone, body=%wide.region_12.14_spmd.clone.clone.sunk | while | flops 62274 | bytes 102632 | solution.py:58
  539.2 4.0 collective-permute-start.4
  543.3 102.9 %psum.14 = f32[64,64]{1,0:T(8,128)S(1)} all-reduce(f32[64,64]{1,0:T(8,128)S(1)} %broadcast_select_fusion.12), channel_id=1, replica_groups=mesh['row'=32,'col'=16] {'row'}, use_global_device_ids=true, to_apply=%region_21.22 | all-reduce | flops 4096 | bytes 32768 | tf_op jit(solution)/shard_map/psum | solution.py:39
  646.6 95.3 %while.164 = (s32[]{:T(128)}, f32[64,64]{1,0:T(8,128)S(1)}, f32[64,64]{0,1:T(8,128)S(1)}, s32[]{:T(128)}, s32[]{:T(128)}) while((s32[]{:T(128)}, f32[64,64]{1,0:T(8,128)S(1)}, f32[64,64]{0,1:T(8,128)S(1)}, s32[]{:T(128)}, s32[]{:T(128)}) %tuple.382), condition=%wide.region_17.18_spmd.clone.clone, body=%wide.region_15.17_spmd.clone.clone.sunk | while | flops 62274 | bytes 102632 | solution.py:58
  742.0 95.1 %while.165 = (s32[]{:T(128)}, f32[64,64]{1,0:T(8,128)S(1)}, f32[64,64]{1,0:T(8,128)S(1)}, s32[]{:T(128)}, s32[]{:T(128)}, /*index=5*/s32[]{:T(128)}, s32[]{:T(128)}) while((s32[]{:T(128)}, f32[64,64]{1,0:T(8,128)S(1)}, f32[64,64]{1,0:T(8,128)S(1)}, s32[]{:T(128)}, s32[]{:T(128)}, /*index=5*/s32[]{:T(128)}, ...), condition=%wide.region_20.21_spmd.clone.clone, body=%wide.region_18.20_spmd.clone.clone.sunk | while | flops 62086 | bytes 69153 | solution.py:77
  837.4 100.7 %while.158 = (s32[]{:T(128)}, f32[64,64]{0,1:T(8,128)S(1)}, f32[64,64]{0,1:T(8,128)S(1)}, s32[]{:T(128)}) while((s32[]{:T(128)}, f32[64,64]{0,1:T(8,128)S(1)}, f32[64,64]{0,1:T(8,128)S(1)}, s32[]{:T(128)}) %tuple.388), condition=%wide.region_24.25_spmd.clone.clone, body=%wide.region_22.24_spmd.clone.clone.sunk | while | flops 16897 | bytes 69965 | solution.py:96
  938.2 95.1 %while.166 = (s32[]{:T(128)}, f32[64,64]{1,0:T(8,128)S(1)}, f32[64,64]{1,0:T(8,128)S(1)}, s32[]{:T(128)}, s32[]{:T(128)}, /*index=5*/s32[]{:T(128)}, s32[]{:T(128)}) while((s32[]{:T(128)}, f32[64,64]{1,0:T(8,128)S(1)}, f32[64,64]{1,0:T(8,128)S(1)}, s32[]{:T(128)}, s32[]{:T(128)}, /*index=5*/s32[]{:T(128)}, ...), condition=%wide.region_27.28_spmd.clone.clone, body=%wide.region_25.27_spmd.clone.clone.sunk | while | flops 62086 | bytes 69153 | solution.py:77
  1033.9 1.5 convolution_bitcast_fusion.9
  1036.2 98.6 %while.167 = (s32[]{:T(128)}, f32[64,64]{1,0:T(8,128)S(1)}, f32[64,64]{1,0:T(8,128)S(1)}, s32[]{:T(128)}, s32[]{:T(128)}, /*index=5*/s32[]{:T(128)}, s32[]{:T(128)}) while((s32[]{:T(128)}, f32[64,64]{1,0:T(8,128)S(1)}, f32[64,64]{1,0:T(8,128)S(1)}, s32[]{:T(128)}, s32[]{:T(128)}, /*index=5*/s32[]{:T(128)}, ...), condition=%wide.region_31.32_spmd.clone.clone, body=%wide.region_29.31_spmd.clone.clone.sunk | while | flops 62086 | bytes 69153 | solution.py:77
  1135.1 50.3 %all-reduce.2.cloned.1.call-done = f32[768,64]{0,1:T(8,128)} async-done(((f32[768,64]{0,1:T(8,128)}), f32[768,64]{0,1:T(8,128)}) %all-reduce.2.cloned.1.call-update) | async-done | bytes 196624 | tf_op jit(solution)/shard_map/psum | solution.py:139
  1186.6 62.0 %all-gather.3.cloned.1.call-done = f32[12288,64]{0,1:T(8,128)} async-done(((f32[384,64]{0,1:T(8,128)}), f32[12288,64]{0,1:T(8,128)}) %all-gather.3.cloned.1.call-update) | async-done | bytes 3145744 | tf_op jit(solution)/shard_map/all_gather | solution.py:132
  1249.9 3.5 collective-permute-start.5
  1253.4 2.3 collective-permute-done.5
  1255.8 4.4 collective-permute-start.6
  1260.2 2.2 collective-permute-done.6
  1262.5 7.6 collective-permute-start.7
  1270.1 2.1 collective-permute-done.7
  1272.2 14.0 %collective-permute-start.8 = (f32[64,64]{1,0:T(8,128)S(1)}, f32[64,64]{1,0:T(8,128)S(1)}, u32[]{:S(2)}, u32[]{:S(2)}) collective-permute-start(f32[64,64]{1,0:T(8,128)S(1)} %add.361), channel_id=1, source_target_pairs={{0,8},{1,9},{2,10},{3,11},{4,12},{5,13},{6,14},{7,15},{8,0},{9,1},... | collective-permute-start | bytes 49160 | tf_op jit(solution)/shard_map/ppermute | solution.py:18
  1286.2 1.9 collective-permute-done.8
  1289.4 77.7 %all-gather.5.cloned.1.call-done = f32[12288,64]{0,1:T(8,128)} async-done(((f32[768,64]{0,1:T(8,128)}), f32[12288,64]{0,1:T(8,128)}) %all-gather.5.cloned.1.call-update) | async-done | bytes 3145744 | tf_op jit(solution)/shard_map/all_gather | solution.py:145
  1368.0 3.1 convolution_subtract_fusion
  (3082 shorter events, 730.5 us)
Async XLA Ops:
  7.2 104.6 %slice-start = ((f32[384,64]{0,1:T(8,128)}), f32[64,64]{0,1:T(8,128)S(1)}, s32[]{:S(2)}) async-start(f32[384,64]{0,1:T(8,128)} %param.23), calls=%async_computation.3 | async-start | bytes 65536 | tf_op jit(solution)/shard_map/slice | solution.py:108
  7.2 1178.1 %all-reduce.2.cloned.1.call-start = ((), (), s32[]{:S(2)}) async-start(), calls=%async_computation | async-start | bytes 393216 | tf_op jit(solution)/shard_map/psum | solution.py:139
  109.8 3.1 collective-permute-start
  214.7 5.8 collective-permute-start.1
  322.3 7.3 collective-permute-start.2
  431.4 6.0 collective-permute-start.3
  539.2 107.0 %collective-permute-start.4 = (f32[64,64]{0,1:T(8,128)S(1)}, f32[64,64]{0,1:T(8,128)S(1)}, u32[]{:S(2)}, u32[]{:S(2)}) collective-permute-start(f32[64,64]{0,1:T(8,128)S(1)} %negate_bitcast_fusion.1), channel_id=1, source_target_pairs={{0,256},{256,0},{16,272},{272,16},{32,288},{288,32},{48,304},{304,... | collective-permute-start | bytes 49160 | tf_op jit(solution)/shard_map/ppermute | solution.py:34
  742.0 291.3 %copy-start.3 = (f32[384,64]{0,1:T(8,128)S(1)}, f32[384,64]{0,1:T(8,128)}, u32[]{:S(2)}) copy-start(f32[384,64]{0,1:T(8,128)} %param.23) | copy-start | bytes 294916
  742.0 291.9 %copy-start = (f32[384,768]{1,0:T(8,128)S(1)}, f32[384,768]{1,0:T(8,128)}, u32[]{:S(2)}) copy-start(f32[384,768]{1,0:T(8,128)} %param.22) | copy-start | bytes 3538948
  837.1 196.8 %copy-start.4 = (f32[64,64]{1,0:T(8,128)}, f32[64,64]{1,0:T(8,128)S(1)}, u32[]{:S(2)}) copy-start(f32[64,64]{1,0:T(8,128)S(1)} %get-tuple-element.1724) | copy-start | bytes 49156
  1033.9 1.6 copy-start.1
  1035.4 213.2 %all-gather.3.cloned.1.call-start = ((), (), s32[]{:S(2)}) async-start(), calls=%async_computation.1 | async-start | bytes 3244032 | tf_op jit(solution)/shard_map/all_gather | solution.py:132
  1036.2 330.9 %all-gather.5.cloned.1.call-start = ((), (), s32[]{:S(2)}) async-start(), calls=%async_computation.2 | async-start | bytes 3342336 | tf_op jit(solution)/shard_map/all_gather | solution.py:145
  1186.6 181.4 %copy-start.2 = (f32[384,64]{0,1:T(8,128)S(1)}, f32[384,64]{0,1:T(8,128)}, u32[]{:S(2)}) copy-start(f32[384,64]{0,1:T(8,128)} %copy-done.1) | copy-start | bytes 294916
  1249.9 5.8 collective-permute-start.5
  1255.8 6.7 collective-permute-start.6
  1262.5 9.7 collective-permute-start.7
  1272.2 15.9 %collective-permute-start.8 = (f32[64,64]{1,0:T(8,128)S(1)}, f32[64,64]{1,0:T(8,128)S(1)}, u32[]{:S(2)}, u32[]{:S(2)}) collective-permute-start(f32[64,64]{1,0:T(8,128)S(1)} %add.361), channel_id=1, source_target_pairs={{0,8},{1,9},{2,10},{3,11},{4,12},{5,13},{6,14},{7,15},{8,0},{9,1},... | collective-permute-start | bytes 49160 | tf_op jit(solution)/shard_map/ppermute | solution.py:18
Sparse Core Ops, SparseCore 0:
  1035.5 149.7 all-reduce.1
  1189.1 59.5 all-gather.2
  1289.5 77.4 all-gather.4
